TPU v7x, 128 devices: a whole 4x4x4 slice. The times are simulated.
128 devices in a mesh: clu: 8 (over x, core), vol: 16 (over y, z).
Axes of the slice: x: 4, y: 4, z: 4, core: 2. Of those that a mesh axis runs over, the one named last changes fastest.
Arguments:
- volume_field: bfloat16 [16, 262144], P(None, ('clu', 'vol')), may hold values from -6 to 6
- trace_rows: int32 [1024, 128], P(('clu', 'vol')), may hold values from 0 to 262143, as said below
- near_block: bfloat16 [16384, 128, 128], P(('clu', 'vol')), may hold values from -0.125 to 0.125
- near_source: int32 [16384], P(('clu', 'vol')), may hold values from 0 to 7
- near_offset: int32 [16384], P(('clu', 'vol')), may hold values from 0 to 2
- near_cluster: int32 [16384], P(('clu', 'vol')), may hold values from 0 to 7
- far_v: bfloat16 [32768, 32, 128], P(('clu', 'vol')), may hold values from -0.5 to 0.5
- far_u: bfloat16 [32768, 32, 128], P(('clu', 'vol')), may hold values from -0.1875 to 0.1875
- far_source: int32 [32768], P(('clu', 'vol')), may hold values from 0 to 7
- far_owner: int32 [32768, 1], P(('clu', 'vol')), may hold values from 0 to 127; in each aligned block of 256 rows (0 to 255, 256 to 511, ...) at most 4 rows name the same one
- far_cluster: int32 [32768], P(('clu', 'vol')), may hold values from 0 to 7
Outputs:
- stray_trace: float32 [1024, 16, 128], P(('clu', 'vol'))
Inputs may be any that keep to these rules, and one draw needn't show every extreme that they name: `trace_rows`: A node of cluster c reads a volume row r with r // 32768 == c // 128; the first and last row of each such range are read. `far_owner`: in the rows of one device (aligned blocks of 256 rows) no owner is named more than 4 times.
All inputs are finite; a program needn't handle non-finite values.
Results may differ from a plain program's by a relative error of at most 0.0021.
Values may be sent and summed in bfloat16 or wider, within the bound.
A program may use at most 64 MiB of HBM per device.

v0:
```python
import jax
import jax.numpy as jnp
from jax import lax
from jax.sharding import PartitionSpec as P


def shifted(value, axis, steps):
    count = lax.axis_size(axis)
    pairs = [(source, (source + steps) % count) for source in range(count)]
    return lax.ppermute(value, axis, pairs)


def body(
    volume_field,
    trace_rows,
    near_block,
    near_source,
    near_offset,
    near_cluster,
    far_v,
    far_u,
    far_source,
    far_owner,
    far_cluster,
):
    clusters, leaf = trace_rows.shape
    modes = volume_field.shape[0]
    devices = lax.axis_size(("clu", "vol"))
    vol_count = lax.axis_size("vol")
    group_rows = volume_field.shape[1] * vol_count
    wanted = trace_rows.reshape(-1) - lax.axis_index("clu") * group_rows
    initial = jnp.zeros((modes, clusters * leaf), jnp.bfloat16)
    piece = lax.all_gather(volume_field, "vol", axis=1, tiled=True)
    width = piece.shape[1]
    inside = (wanted >= 0) & (wanted < width)
    taken = jnp.take(piece, jnp.clip(wanted, 0, width - 1), axis=1)
    values = jnp.where(inside[None, :], taken, initial)
    boundary = values.reshape(modes, clusters, leaf).transpose(1, 0, 2)
    width = modes * leaf
    near_in = boundary[near_source]
    near_terms = jnp.einsum("pij,pvj->pvi", near_block, near_in, preferred_element_type=jnp.float32)
    near_pairs = near_terms.shape[0]
    group_ids = near_offset * clusters + near_cluster
    selector = (group_ids[None, :] == jnp.arange(3 * clusters, dtype=jnp.int32)[:, None]).astype(
        jnp.float32
    )
    grouped = jnp.dot(
        selector, near_terms.reshape(near_pairs, width), precision=lax.Precision.HIGHEST
    )
    grouped = grouped.reshape(3, clusters, width)
    from_before = shifted(grouped[2], ("clu", "vol"), 1)
    from_after = shifted(grouped[0], ("clu", "vol"), -1)
    near_total = grouped[1] + from_before + from_after
    far_in = boundary[far_source]
    coeff = jnp.einsum("prl,pvl->prv", far_v, far_in, preferred_element_type=jnp.float32).astype(
        jnp.bfloat16
    )
    far_terms = jnp.einsum("prv,prl->pvl", coeff, far_u, preferred_element_type=jnp.float32)
    far_pairs = far_terms.shape[0]
    far_flat = far_terms.reshape(far_pairs, width)
    owner = far_owner[:, 0]
    target_ids = owner * clusters + far_cluster
    dense_terms = jax.ops.segment_sum(far_flat, target_ids, num_segments=devices * clusters)
    received = lax.psum_scatter(dense_terms, ("clu", "vol"), scatter_dimension=0, tiled=True)
    total = near_total + received
    return total.reshape(clusters, modes, leaf)


def solution(mesh):
    return jax.shard_map(
        body,
        mesh=mesh,
        in_specs=(
            P(None, ("clu", "vol")),
            P(("clu", "vol"), None),
            P(("clu", "vol"), None, None),
            P(("clu", "vol")),
            P(("clu", "vol")),
            P(("clu", "vol")),
            P(("clu", "vol"), None, None),
            P(("clu", "vol"), None, None),
            P(("clu", "vol")),
            P(("clu", "vol"), None),
            P(("clu", "vol")),
        ),
        out_specs=P(("clu", "vol"), None, None),
        check_vma=False,
    )
```

profile of v0, /device:TPU:0, one launch (start us, length us, event | category | flops | bytes accessed | tf_op | source)
XLA Modules:
  0.0 764.4 jit_solution(9761731943342545036)
XLA Ops:
  6.5 0.0 copy-start
  6.5 0.0 all-gather.2.cloned.1.call-start
  6.5 2.0 copy.14
  8.6 0.0 all-gather.2.cloned.1.call-update
  8.6 0.0 reduce-scatter.2.cloned.1.call-start
  8.6 0.7 broadcast_multiply_fusion
  9.3 0.7 add.49
  10.0 0.7 compare_select_fusion.2
  10.7 0.7 compare_and_fusion
  11.4 71.4 %all-gather.2.cloned.1.call-done = bf16[16,32768]{0,1:T(8,128)(2,1)} async-done(((bf16[16,2048]{0,1:T(8,128)(2,1)}), bf16[16,32768]{0,1:T(8,128)(2,1)}) %all-gather.2.cloned.1.call-update) | async-done | bytes 1048592 | tf_op jit(solution)/shard_map/all_gather | solution.py:33
  82.9 7.3 gather_fusion
  90.2 0.1 copy.15
  90.4 0.9 gather_fusion.2
  91.2 0.0 copy-done
  91.2 4.7 fusion.4
  95.9 9.1 %scatter_custom_fusion = f32[1024,2048]{1,0:T(8,128)} fusion(s32[256]{0:T(256)S(1)} %add.49, f32[]{:T(128)} %constant.17.clone.1, f32[32,8,16,128]{3,2,1,0:T(8,128)} %bitcast.23), kind=kCustom, calls=%fused_computation.4 | custom fusion | flops 524288 | bytes 10485764 | tf_op jit(solution)/shard_map/scatter-add | solution.py:63
  105.1 0.0 copy-start.1
  105.1 0.0 copy-start.2
  105.1 0.0 copy-start.3
  105.1 0.0 reduce-scatter.2.cloned.1.call-update
  105.1 0.6 copy-done.1
  105.8 0.0 copy-done.2
  105.8 0.0 copy-done.3
  105.8 0.7 gather_fusion.1
  106.5 4.5 fusion.13
  110.9 0.8 fusion.5
  111.7 4.6 collective-permute-start.1
  116.4 0.0 collective-permute-start
  116.4 1.9 collective-permute-done.1
  118.3 7.2 collective-permute-done
  125.5 630.5 %reduce-scatter.2.cloned.1.call-done = f32[8,2048]{1,0:T(8,128)} async-done(((f32[1024,2048]{1,0:T(8,128)}), f32[8,2048]{1,0:T(8,128)}) %reduce-scatter.2.cloned.1.call-update) | async-done | bytes 65552 | tf_op jit(solution)/shard_map/reduce_scatter | solution.py:64
  756.0 0.9 fusion.10
  756.9 0.6 copy.16
  (8 shorter events, 0.1 us)
Async XLA Ops:
  6.5 84.7 %copy-start = (bf16[256,32,128]{2,1,0:T(8,128)(2,1)S(1)}, bf16[256,32,128]{2,1,0:T(8,128)(2,1)}, u32[]{:S(2)}) copy-start(bf16[256,32,128]{2,1,0:T(8,128)(2,1)} %param.18) | copy-start | bytes 6291460
  6.5 76.3 %all-gather.2.cloned.1.call-start = ((), (), s32[]{:S(2)}) async-start(), calls=%async_computation.1 | async-start | bytes 8912896 | tf_op jit(solution)/shard_map/all_gather | solution.py:33
  8.6 747.4 %reduce-scatter.2.cloned.1.call-start = ((), (), s32[]{:S(2)}) async-start(), calls=%async_computation.2 | async-start | bytes 8454144 | tf_op jit(solution)/shard_map/reduce_scatter | solution.py:64
  105.1 0.7 copy-start.1
  105.1 0.7 copy-start.2
  105.1 0.7 copy-start.3
  111.7 6.6 collective-permute-start.1
  116.4 9.1 %collective-permute-start = (f32[8,2048]{1,0:T(8,128)S(1)}, f32[8,2048]{1,0:T(8,128)S(1)}, u32[]{:S(2)}, u32[]{:S(2)}) collective-permute-start(f32[8,2048]{1,0:T(8,128)S(1)} %get-tuple-element.7), channel_id=1, source_target_pairs={{0,1},{1,2},{2,3},{3,4},{4,5},{5,6},{6,7},{7,8},{8,9},{9,10},{10,1... | collective-permute-start | bytes 196616 | tf_op jit(solution)/shard_map/ppermute | solution.py:10
Sparse Core Ops, SparseCore 0:
  9.5 73.3 all-gather.1
  105.2 650.7 reduce-scatter.1
where the time goes:
time: 765 us; the launch traced here: 764 us
  waiting for transfers between devices  711 us (93%)
  between operations  13.5 us (2%)
  other arithmetic  12.8 us (2%)
  local copies, waits for them, and re-layouts  12.3 us (2%)
  matrix products  9.93 us (1%)
    reduce_scatter x1, waiting for transfers between devices, body(): lax.psum_scatter(dense_terms, ('clu', 'vol'), scatter_dimension=0, tiled=...  631 us
    all_gather x1, waiting for transfers between devices, body(): piece = lax.all_gather(volume_field, 'vol', axis=1, tiled=True)  71.4 us
  transfers between devices with their start and end apart: 4, of which 4 were waited for; matrix products, arithmetic and copies ran while one was open for 1% of the time, Pallas kernels for 0%

commit v1 on v0

v1 whole, which is shorter than its diff:
```python
import jax
import jax.numpy as jnp
from jax import lax
from jax.experimental import pallas as pl
from jax.experimental.pallas import tpu as pltpu
from jax.sharding import PartitionSpec as P

MESH = pl.DeviceIdType.MESH
F32 = jnp.float32
BF16 = jnp.bfloat16
NT = (((1,), (1,)), ((), ()))

LEAF = 128
NVEC = 16
NDEV = 128
CLUSTERS = 8
SLOTS = 4
NEAR = 128
FAR = 256
RANK = 32
STEPS = 16
PER_STEP = NDEV // STEPS
TILES = 256


def iota(shape, dim):
    return lax.broadcasted_iota(jnp.int32, shape, dim)


def place():
    clu, vol = lax.axis_index("clu"), lax.axis_index("vol")
    return clu // 2, clu % 2, vol // 4, vol % 4


def device(x, core, y, z):
    return (x % 4) * 2 + core % 2, (y % 4) * 4 + z % 4


def partner(k):
    x, core, y, z = place()
    m = (k * 37) % NDEV
    r = m // 2
    clu, vol = device(x + r % 4, core + m % 2, y + (r // 4) % 4, z + r // 16)
    return (clu, vol), clu * 16 + vol


def kernel(
    vol_ref,
    rows_ref,
    nsrc_ref,
    noff_ref,
    nclu_ref,
    fsrc_ref,
    fown_ref,
    fclu_ref,
    near_hbm,
    fv_hbm,
    fu_hbm,
    out_ref,
    table,
    near_vm,
    fv_vm,
    fu_vm,
    bound,
    terms,
    send,
    recv,
    idx_vm,
    idx_sm,
    ids_send,
    ids_recv,
    masks,
    nterm_hi,
    nterm_lo,
    nsum,
    nrecv,
    load_sem,
    idx_sem,
    tab_send,
    tab_recv,
    ids_ssem,
    ids_rsem,
    send_sem,
    recv_sem,
    near_ssem,
    near_rsem,
):
    x, core, y, z = place()
    clu, vol = lax.axis_index("clu"), lax.axis_index("vol")

    loads = [
        pltpu.make_async_copy(fv_hbm, fv_vm, load_sem.at[0]),
        pltpu.make_async_copy(fu_hbm, fu_vm, load_sem.at[1]),
        pltpu.make_async_copy(near_hbm, near_vm, load_sem.at[2]),
    ]
    for load in loads:
        load.start()

    barrier = pltpu.get_barrier_semaphore()

    def greet(k, carry):
        pl.semaphore_signal(barrier, inc=1, device_id=partner(k)[0], device_id_type=MESH)
        return carry

    lax.fori_loop(1, NDEV, greet, 0)

    base = vol * 16
    for hi in range(16):
        table[base + hi] = vol_ref[:, hi * LEAF : (hi + 1) * LEAF]

    owns = iota((NDEV, FAR), 0) == fown_ref[...]
    upto = (iota((FAR, FAR), 0) <= iota((FAR, FAR), 1)).astype(F32).astype(BF16)
    count = jnp.dot(owns.astype(F32).astype(BF16), upto, preferred_element_type=F32)
    number = (iota((16, FAR), 1) + 1).astype(F32).astype(BF16)
    clusters = fclu_ref[...].astype(F32)
    slot_of_lane = (iota((NDEV, LEAF), 1) // NVEC) % SLOTS
    ids = jnp.zeros((NDEV, LEAF), F32)
    for j in range(SLOTS):
        chosen = jnp.where(owns & (count == float(j + 1)), 1.0, 0.0)
        found = lax.dot_general(number, chosen.astype(BF16), NT, preferred_element_type=F32)
        idx_vm[j : j + 1, :] = found[0:1, :].astype(jnp.int32)
        target = jnp.sum(chosen * clusters, axis=1, keepdims=True)
        ids = jnp.where(slot_of_lane == j, target, ids)
    ids_send[...] = ids.reshape(NDEV, 1, LEAF)
    to_smem = pltpu.make_async_copy(idx_vm, idx_sm, idx_sem)
    to_smem.start()

    pl.semaphore_wait(barrier, NDEV - 1)

    def half(dy, dz, h):
        owner = ((y - dy + 4) % 4) * 4 + (z - dz + 4) % 4
        return table.at[pl.ds(owner * 16 + h * 8, 8)]

    def pass_on(dy, dz, h, ey, ez):
        block = half(dy, dz, h)
        pltpu.make_async_remote_copy(
            src_ref=block,
            dst_ref=block,
            send_sem=tab_send,
            recv_sem=tab_recv.at[h * 16 + (dy + ey) * 4 + dz + ez],
            device_id=(clu, ((y + ey) % 4) * 4 + (z + ez) % 4),
            device_id_type=MESH,
        ).start()

    def arrived(dy, dz, h):
        block = half(dy, dz, h)
        pltpu.make_async_copy(block, block, tab_recv.at[h * 16 + dy * 4 + dz]).wait()

    order = (1, 3, 2)
    for e in order:
        pass_on(0, 0, 0, 0, e)
        pass_on(0, 0, 1, e, 0)
    for e in order:
        pass_on(0, 0, 0, e, 0)
        pass_on(0, 0, 1, 0, e)

    def send_ids(k, carry):
        dev, flat = partner(k)
        pltpu.make_async_remote_copy(
            src_ref=ids_send.at[flat],
            dst_ref=ids_recv.at[k],
            send_sem=ids_ssem,
            recv_sem=ids_rsem,
            device_id=dev,
            device_id_type=MESH,
        ).start()
        return carry

    for d in order:
        arrived(0, d, 0)
        for e in order:
            pass_on(0, d, 0, e, 0)
        arrived(d, 0, 1)
        for e in order:
            pass_on(d, 0, 1, 0, e)
    lax.fori_loop(1, NDEV, send_ids, 0)
    ids_recv[0] = ids_send[clu * 16 + vol]

    for d in order:
        arrived(d, 0, 0)
        arrived(0, d, 1)
    for d in order:
        for e in order:
            arrived(d, e, 0)
            arrived(d, e, 1)

    lane = iota((NVEC, LEAF), 1)

    def gather(c, carry):
        got = jnp.zeros((NVEC, LEAF), F32)
        for n in range(LEAF):
            row = rows_ref[c, n] & (TILES * LEAF - 1)
            tile = table[lax.shift_right_logical(row, 7)].astype(F32)
            got = jnp.where(lane == n, pltpu.roll(tile, (n - row) & (LEAF - 1), axis=1), got)
        bound[c] = got.astype(BF16)
        return carry

    lax.fori_loop(0, CLUSTERS, gather, 0)

    loads[0].wait()
    loads[1].wait()
    same = iota((8 * NVEC, 8 * RANK), 0) // NVEC == iota((8 * NVEC, 8 * RANK), 1) // RANK
    terms[0] = jnp.zeros((NVEC, LEAF), BF16)

    def far(g, carry):
        first = g * 8
        lhs = jnp.concatenate([bound[fsrc_ref[first + i]] for i in range(8)], axis=0)
        v = fv_vm[pl.ds(first, 8)].reshape(8 * RANK, LEAF)
        u = fu_vm[pl.ds(first, 8)].reshape(8 * RANK, LEAF)
        coeff = lax.dot_general(lhs, v, NT, preferred_element_type=F32)
        coeff = jnp.where(same, coeff, 0.0).astype(BF16)
        term = jnp.dot(coeff, u, preferred_element_type=F32)
        terms[pl.ds(first + 1, 8)] = term.astype(BF16).reshape(8, NVEC, LEAF)
        return carry

    lax.fori_loop(0, FAR // 8, far, 0)

    to_smem.wait()
    me = clu * 16 + vol
    for j in range(SLOTS):
        recv[0, j * NVEC : (j + 1) * NVEC, :] = terms[jnp.clip(idx_sm[j, me], 0, FAR)]

    def send_terms(k, carry):
        dev, flat = partner(k)
        for j in range(SLOTS):
            send[k, j * NVEC : (j + 1) * NVEC, :] = terms[jnp.clip(idx_sm[j, flat], 0, FAR)]
        pltpu.make_async_remote_copy(
            src_ref=send.at[k],
            dst_ref=recv.at[k],
            send_sem=send_sem,
            recv_sem=recv_sem.at[k // PER_STEP],
            device_id=dev,
            device_id_type=MESH,
        ).start()
        return carry

    lax.fori_loop(1, NDEV, send_terms, 0)

    loads[2].wait()

    def near(g, carry):
        first = g * 8
        for i in range(8):
            term = lax.dot_general(bound[nsrc_ref[first + i]], near_vm[first + i], NT, preferred_element_type=F32)
            high = term.astype(BF16)
            nterm_hi[first + i] = high
            nterm_lo[first + i] = (term - high.astype(F32)).astype(BF16)
        return carry

    lax.fori_loop(0, NEAR // 8, near, 0)

    rows = 3 * CLUSTERS * NVEC
    named = (noff_ref[...] * CLUSTERS + nclu_ref[...]).astype(F32).astype(BF16)
    named = jnp.broadcast_to(named, (16, NEAR))
    vec_row = iota((rows, 256), 0) % NVEC == iota((rows, 256), 1) % NVEC
    target_row = (iota((rows, 256), 0) // NVEC).astype(F32)
    nsum[...] = jnp.zeros_like(nsum)

    def near_sum(g, carry):
        first = g * 16
        spread = (iota((NEAR, 256), 0) == first + iota((NEAR, 256), 1) // NVEC).astype(F32).astype(BF16)
        wanted = jnp.dot(named, spread, preferred_element_type=F32)[0:1, :]
        pick = jnp.where(vec_row & (target_row == wanted), 1.0, 0.0).astype(BF16)
        high = nterm_hi[pl.ds(first, 16)].reshape(256, LEAF)
        low = nterm_lo[pl.ds(first, 16)].reshape(256, LEAF)
        total = jnp.dot(pick, high, preferred_element_type=F32) + jnp.dot(pick, low, preferred_element_type=F32)
        nsum[...] += total.reshape(3 * CLUSTERS, NVEC, LEAF)
        return carry

    lax.fori_loop(0, NEAR // 16, near_sum, 0)

    before, after = (me + NDEV - 1) % NDEV, (me + 1) % NDEV
    near_copies = []
    for i, (block, to) in enumerate(((0, before), (2, after))):
        copy = pltpu.make_async_remote_copy(
            src_ref=nsum.at[pl.ds(block * CLUSTERS, CLUSTERS)],
            dst_ref=nrecv.at[i],
            send_sem=near_ssem.at[i],
            recv_sem=near_rsem.at[i],
            device_id=(to // 16, to % 16),
            device_id_type=MESH,
        )
        copy.start()
        near_copies.append(copy)

    pltpu.make_async_copy(ids_recv.at[pl.ds(1, NDEV - 1)], ids_recv.at[pl.ds(1, NDEV - 1)], ids_rsem).wait()
    vec_same = iota((LEAF, LEAF), 0) % NVEC == iota((LEAF, LEAF), 1) % NVEC
    cluster_row = (iota((LEAF, LEAF), 0) // NVEC).astype(F32)
    left = iota((1, LEAF), 1) < LEAF // 2

    def make_mask(g, carry):
        wanted = jnp.where(left, ids_recv[g * 2], ids_recv[g * 2 + 1])
        masks[g] = jnp.where(vec_same & (cluster_row == wanted), 1.0, 0.0).astype(BF16)
        return carry

    lax.fori_loop(0, NDEV // 2, make_mask, 0)

    total = nsum[pl.ds(CLUSTERS, CLUSTERS)].reshape(CLUSTERS * NVEC, LEAF)
    for s in range(STEPS):
        lo = max(1, s * PER_STEP)
        part = recv.at[pl.ds(lo, (s + 1) * PER_STEP - lo)]
        pltpu.make_async_copy(part, part, recv_sem.at[s]).wait()
        for t in range(PER_STEP // 4):
            g = s * PER_STEP // 2 + t * 2
            pick = jnp.concatenate([masks[g], masks[g + 1]], axis=1)
            block = recv[pl.ds(g * 2, 4)].reshape(4 * SLOTS * NVEC, LEAF)
            total += jnp.dot(pick, block, preferred_element_type=F32)
    for copy in near_copies:
        copy.wait()
    total = total.reshape(CLUSTERS, NVEC, LEAF)
    out_ref[...] = total + nrecv[0] + nrecv[1]

    sent = table.at[pl.ds(0, 240)]
    pltpu.make_async_copy(sent, sent, tab_send).wait()
    sent = ids_send.at[pl.ds(1, NDEV - 1)]
    pltpu.make_async_copy(sent, sent, ids_ssem).wait()
    sent = send.at[pl.ds(1, NDEV - 1)]
    pltpu.make_async_copy(sent, sent, send_sem).wait()


def body(
    volume_field,
    trace_rows,
    near_block,
    near_source,
    near_offset,
    near_cluster,
    far_v,
    far_u,
    far_source,
    far_owner,
    far_cluster,
):
    vmem = pl.BlockSpec(memory_space=pltpu.VMEM)
    smem = pl.BlockSpec(memory_space=pltpu.SMEM)
    hbm = pl.BlockSpec(memory_space=pl.ANY)
    dma = pltpu.SemaphoreType.DMA
    return pl.pallas_call(
        kernel,
        out_shape=jax.ShapeDtypeStruct((CLUSTERS, NVEC, LEAF), F32),
        in_specs=[vmem, smem, smem, vmem, vmem, smem, vmem, vmem, hbm, hbm, hbm],
        out_specs=vmem,
        scratch_shapes=[
            pltpu.VMEM((TILES, NVEC, LEAF), BF16),
            pltpu.VMEM((NEAR, LEAF, LEAF), BF16),
            pltpu.VMEM((FAR, RANK, LEAF), BF16),
            pltpu.VMEM((FAR, RANK, LEAF), BF16),
            pltpu.VMEM((CLUSTERS, NVEC, LEAF), BF16),
            pltpu.VMEM((FAR + 8, NVEC, LEAF), BF16),
            pltpu.VMEM((NDEV, SLOTS * NVEC, LEAF), BF16),
            pltpu.VMEM((NDEV, SLOTS * NVEC, LEAF), BF16),
            pltpu.VMEM((8, NDEV), jnp.int32),
            pltpu.SMEM((8, NDEV), jnp.int32),
            pltpu.VMEM((NDEV, 1, LEAF), F32),
            pltpu.VMEM((NDEV, 1, LEAF), F32),
            pltpu.VMEM((NDEV // 2, LEAF, LEAF), BF16),
            pltpu.VMEM((NEAR, NVEC, LEAF), BF16),
            pltpu.VMEM((NEAR, NVEC, LEAF), BF16),
            pltpu.VMEM((3 * CLUSTERS, NVEC, LEAF), F32),
            pltpu.VMEM((2, CLUSTERS, NVEC, LEAF), F32),
            dma((3,)),
            dma,
            dma,
            dma((32,)),
            dma,
            dma,
            dma,
            dma((STEPS,)),
            dma((2,)),
            dma((2,)),
        ],
        compiler_params=pltpu.CompilerParams(
            collective_id=0, has_side_effects=True, vmem_limit_bytes=40 * 2**20
        ),
        cost_estimate=pl.CostEstimate(flops=2 * 10**8, bytes_accessed=9 * 2**20, transcendentals=0),
    )(
        volume_field,
        trace_rows,
        near_source,
        near_offset.reshape(1, NEAR),
        near_cluster.reshape(1, NEAR),
        far_source,
        far_owner.reshape(1, FAR),
        far_cluster.reshape(1, FAR),
        near_block,
        far_v,
        far_u,
    )


def solution(mesh):
    both = ("clu", "vol")
    return jax.shard_map(
        body,
        mesh=mesh,
        in_specs=(
            P(None, both),
            P(both, None),
            P(both, None, None),
            P(both),
            P(both),
            P(both),
            P(both, None, None),
            P(both, None, None),
            P(both),
            P(both, None),
            P(both),
        ),
        out_specs=P(both, None, None),
        check_vma=False,
    )
```

time: 765 us -> 78.6 us (0.10)
  the two profiles are of different devices: /device:TPU:0 before, /device:TPU:1 now
where the time goes in v1:
time: 78.6 us; the launch traced here: 78.3 us
  Pallas kernels  66.7 us (85%)
  local copies, waits for them, and re-layouts  11.5 us (15%)
    pallas_call x1, Pallas kernels, body(): pl.pallas_call(kernel, out_shape=jax.ShapeDtypeStruct((CLUSTERS, NVEC, LE...  66.7 us
    unnamed x23, local copies, waits for them, and re-layouts  11.5 us

profile of v1, /device:TPU:1, one launch (start us, length us, event | category | flops | bytes accessed | tf_op | source)
XLA Modules:
  0.0 78.3 jit_solution(5037191739764358703)
XLA Ops:
  0.0 0.0 copy-start
  0.0 2.2 %copy-done = bf16[128,128,128]{2,1,0:T(8,128)(2,1)S(1)} copy-done((bf16[128,128,128]{2,1,0:T(8,128)(2,1)S(1)}, bf16[128,128,128]{2,1,0:T(8,128)(2,1)}, u32[]{:S(2)}) %copy-start) | copy-done | bytes 4194328
  2.2 0.0 copy-start.1
  2.2 1.6 %copy-done.1 = bf16[256,32,128]{2,1,0:T(8,128)(2,1)S(1)} copy-done((bf16[256,32,128]{2,1,0:T(8,128)(2,1)S(1)}, bf16[256,32,128]{2,1,0:T(8,128)(2,1)}, u32[]{:S(2)}) %copy-start.1) | copy-done | bytes 2097176
  3.8 0.0 copy-start.2
  3.8 1.6 %copy-done.2 = bf16[256,32,128]{2,1,0:T(8,128)(2,1)S(1)} copy-done((bf16[256,32,128]{2,1,0:T(8,128)(2,1)S(1)}, bf16[256,32,128]{2,1,0:T(8,128)(2,1)}, u32[]{:S(2)}) %copy-start.2) | copy-done | bytes 2097176
  5.4 0.0 copy-start.3
  5.4 0.8 %copy-done.3 = bf16[16,2048]{1,0:T(8,128)(2,1)S(1)} copy-done((bf16[16,2048]{1,0:T(8,128)(2,1)S(1)}, bf16[16,2048]{1,0:T(8,128)(2,1)}, u32[]{:S(2)}) %copy-start.3) | copy-done | bytes 65560
  6.2 0.0 copy-start.4
  6.2 0.7 copy-done.4
  6.9 0.0 copy-start.5
  6.9 0.7 copy-done.5
  7.6 0.0 copy-start.6
  7.6 0.7 copy-done.6
  8.3 0.0 copy-start.7
  8.3 0.7 copy-done.7
  8.9 0.0 copy-start.8
  8.9 0.7 copy-done.8
  9.6 0.0 copy-start.9
  9.6 0.7 copy-done.9
  10.2 0.0 copy-start.10
  10.3 0.7 copy-done.10
  10.9 66.7 %shard_map.109 = f32[8,16,128]{2,1,0:T(8,128)S(1)} custom-call(bf16[16,2048]{1,0:T(8,128)(2,1)S(1)} %copy-done.3, s32[8,128]{1,0:T(8,128)S(1)} %copy-done.4, s32[128]{0:T(128)S(1)} %copy-done.8, s32[1,128]{1,0:T(1,128)S(1)} %bitcast.6, s32[1,128]{1,0:T(1,128)S(1)} %bitcast.7, s32[256]{0:T(256)S(1)} %copy-done.5, s32[1,256]{1,0:T(1,128)S(1)} %bitcast.4, ...), custom_call_target="tpu_custom_call" | custom-call | flops 200000000 | bytes 9437184 | tf_op jit(solution)/shard_map/pallas_call | solution.py:338
  77.6 0.6 copy.13
Async XLA Ops:
  0.0 2.2 %copy-start = (bf16[128,128,128]{2,1,0:T(8,128)(2,1)S(1)}, bf16[128,128,128]{2,1,0:T(8,128)(2,1)}, u32[]{:S(2)}) copy-start(bf16[128,128,128]{2,1,0:T(8,128)(2,1)} %near_hbm.1) | copy-start | bytes 12582916
  2.2 1.6 %copy-start.1 = (bf16[256,32,128]{2,1,0:T(8,128)(2,1)S(1)}, bf16[256,32,128]{2,1,0:T(8,128)(2,1)}, u32[]{:S(2)}) copy-start(bf16[256,32,128]{2,1,0:T(8,128)(2,1)} %fv_hbm.1) | copy-start | bytes 6291460
  3.8 1.6 %copy-start.2 = (bf16[256,32,128]{2,1,0:T(8,128)(2,1)S(1)}, bf16[256,32,128]{2,1,0:T(8,128)(2,1)}, u32[]{:S(2)}) copy-start(bf16[256,32,128]{2,1,0:T(8,128)(2,1)} %fu_hbm.1) | copy-start | bytes 6291460
  5.4 0.8 %copy-start.3 = (bf16[16,2048]{1,0:T(8,128)(2,1)S(1)}, bf16[16,2048]{1,0:T(8,128)(2,1)}, u32[]{:S(2)}) copy-start(bf16[16,2048]{1,0:T(8,128)(2,1)} %vol_ref.1) | copy-start | bytes 196612
  6.2 0.7 copy-start.4
  6.9 0.7 copy-start.5
  7.6 0.7 copy-start.6
  8.3 0.7 copy-start.7
  8.9 0.7 copy-start.8
  9.6 0.7 copy-start.9
  10.2 0.7 copy-start.10

commit v2 on v1

--- a/solution.py
+++ b/solution.py
@@ -29,22 +29,32 @@
 
 def place():
     clu, vol = lax.axis_index("clu"), lax.axis_index("vol")
-    return clu // 2, clu % 2, vol // 4, vol % 4
-
-
-def device(x, core, y, z):
-    return (x % 4) * 2 + core % 2, (y % 4) * 4 + z % 4
-
-
-def partner(k):
+    return lax.div(clu, 2), lax.rem(clu, 2), lax.div(vol, 4), lax.rem(vol, 4)
+
+
+def partner(k, sign):
     x, core, y, z = place()
-    m = (k * 37) % NDEV
-    r = m // 2
-    clu, vol = device(x + r % 4, core + m % 2, y + (r // 4) % 4, z + r // 16)
-    return (clu, vol), clu * 16 + vol
+    m = lax.rem(k * 37, NDEV)
+    r = lax.div(m, 2)
+    dx, dy, dz = lax.rem(r, 4), lax.rem(lax.div(r, 4), 4), lax.div(r, 16)
+    clu = lax.rem(x + 4 + sign * dx, 4) * 2 + lax.rem(core + m, 2)
+    vol = lax.rem(y + 4 + sign * dy, 4) * 4 + lax.rem(z + 4 + sign * dz, 4)
+    return clu, vol
 
 
 def kernel(
+    vol_hbm,
+    rows_hbm,
+    nsrc_hbm,
+    noff_hbm,
+    nclu_hbm,
+    fsrc_hbm,
+    fown_hbm,
+    fclu_hbm,
+    near_hbm,
+    fv_hbm,
+    fu_hbm,
+    out_ref,
     vol_ref,
     rows_ref,
     nsrc_ref,
@@ -53,21 +63,17 @@
     fsrc_ref,
     fown_ref,
     fclu_ref,
-    near_hbm,
-    fv_hbm,
-    fu_hbm,
-    out_ref,
     table,
     near_vm,
     fv_vm,
     fu_vm,
     bound,
-    terms,
     send,
     recv,
     idx_vm,
     idx_sm,
     ids_send,
+    ids_half,
     ids_recv,
     masks,
     nterm_hi,
@@ -80,6 +86,7 @@
     tab_recv,
     ids_ssem,
     ids_rsem,
+    sync,
     send_sem,
     recv_sem,
     near_ssem,
@@ -88,21 +95,37 @@
     x, core, y, z = place()
     clu, vol = lax.axis_index("clu"), lax.axis_index("vol")
 
-    loads = [
-        pltpu.make_async_copy(fv_hbm, fv_vm, load_sem.at[0]),
-        pltpu.make_async_copy(fu_hbm, fu_vm, load_sem.at[1]),
-        pltpu.make_async_copy(near_hbm, near_vm, load_sem.at[2]),
-    ]
+    barrier = pltpu.get_barrier_semaphore()
+
+    def along_clu(k):
+        return lax.rem(clu + k, 8), vol
+
+    def along(ey, ez):
+        return clu, lax.rem(y + ey, 4) * 4 + lax.rem(z + ez, 4)
+
+    near_by = [along_clu(k) for k in range(1, 8)]
+    near_by += [along(e, 0) for e in range(1, 4)] + [along(0, e) for e in range(1, 4)]
+    for dev in near_by:
+        pl.semaphore_signal(barrier, inc=1, device_id=dev, device_id_type=MESH)
+
+    pairs = (
+        (vol_hbm, vol_ref),
+        (fown_hbm, fown_ref),
+        (fclu_hbm, fclu_ref),
+        (rows_hbm, rows_ref),
+        (fsrc_hbm, fsrc_ref),
+        (fv_hbm, fv_vm),
+        (fu_hbm, fu_vm),
+        (nsrc_hbm, nsrc_ref),
+        (noff_hbm, noff_ref),
+        (nclu_hbm, nclu_ref),
+        (near_hbm, near_vm),
+    )
+    loads = [pltpu.make_async_copy(a, b, load_sem.at[i]) for i, (a, b) in enumerate(pairs)]
     for load in loads:
         load.start()
-
-    barrier = pltpu.get_barrier_semaphore()
-
-    def greet(k, carry):
-        pl.semaphore_signal(barrier, inc=1, device_id=partner(k)[0], device_id_type=MESH)
-        return carry
-
-    lax.fori_loop(1, NDEV, greet, 0)
+    for load in loads[:3]:
+        load.wait()
 
     base = vol * 16
     for hi in range(16):
@@ -111,24 +134,24 @@
     owns = iota((NDEV, FAR), 0) == fown_ref[...]
     upto = (iota((FAR, FAR), 0) <= iota((FAR, FAR), 1)).astype(F32).astype(BF16)
     count = jnp.dot(owns.astype(F32).astype(BF16), upto, preferred_element_type=F32)
-    number = (iota((16, FAR), 1) + 1).astype(F32).astype(BF16)
-    clusters = fclu_ref[...].astype(F32)
+    number = iota((16, FAR), 1).astype(F32).astype(BF16)
+    clusters = fclu_ref[...].astype(F32) + 1.0
     slot_of_lane = (iota((NDEV, LEAF), 1) // NVEC) % SLOTS
     ids = jnp.zeros((NDEV, LEAF), F32)
     for j in range(SLOTS):
         chosen = jnp.where(owns & (count == float(j + 1)), 1.0, 0.0)
         found = lax.dot_general(number, chosen.astype(BF16), NT, preferred_element_type=F32)
         idx_vm[j : j + 1, :] = found[0:1, :].astype(jnp.int32)
-        target = jnp.sum(chosen * clusters, axis=1, keepdims=True)
+        target = jnp.sum(chosen * clusters, axis=1, keepdims=True) - 1.0
         ids = jnp.where(slot_of_lane == j, target, ids)
     ids_send[...] = ids.reshape(NDEV, 1, LEAF)
     to_smem = pltpu.make_async_copy(idx_vm, idx_sm, idx_sem)
     to_smem.start()
 
-    pl.semaphore_wait(barrier, NDEV - 1)
+    pl.semaphore_wait(barrier, len(near_by))
 
     def half(dy, dz, h):
-        owner = ((y - dy + 4) % 4) * 4 + (z - dz + 4) % 4
+        owner = lax.rem(y + 4 - dy, 4) * 4 + lax.rem(z + 4 - dz, 4)
         return table.at[pl.ds(owner * 16 + h * 8, 8)]
 
     def pass_on(dy, dz, h, ey, ez):
@@ -138,7 +161,7 @@
             dst_ref=block,
             send_sem=tab_send,
             recv_sem=tab_recv.at[h * 16 + (dy + ey) * 4 + dz + ez],
-            device_id=(clu, ((y + ey) % 4) * 4 + (z + ez) % 4),
+            device_id=along(ey, ez),
             device_id_type=MESH,
         ).start()
 
@@ -154,17 +177,17 @@
         pass_on(0, 0, 0, e, 0)
         pass_on(0, 0, 1, 0, e)
 
-    def send_ids(k, carry):
-        dev, flat = partner(k)
+    for k in range(1, 8):
+        dev = along_clu(k)
         pltpu.make_async_remote_copy(
-            src_ref=ids_send.at[flat],
-            dst_ref=ids_recv.at[k],
-            send_sem=ids_ssem,
-            recv_sem=ids_rsem,
+            src_ref=ids_send.at[pl.ds(dev[0] * 16, 16)],
+            dst_ref=ids_half.at[clu],
+            send_sem=ids_ssem.at[0],
+            recv_sem=ids_rsem.at[0],
             device_id=dev,
             device_id_type=MESH,
         ).start()
-        return carry
+    ids_half[clu] = ids_send[pl.ds(clu * 16, 16)]
 
     for d in order:
         arrived(0, d, 0)
@@ -173,9 +196,6 @@
         arrived(d, 0, 1)
         for e in order:
             pass_on(d, 0, 1, 0, e)
-    lax.fori_loop(1, NDEV, send_ids, 0)
-    ids_recv[0] = ids_send[clu * 16 + vol]
-
     for d in order:
         arrived(d, 0, 0)
         arrived(0, d, 1)
@@ -184,6 +204,24 @@
             arrived(d, e, 0)
             arrived(d, e, 1)
 
+    for k in range(1, 8):
+        pl.semaphore_signal(sync, inc=1, device_id=along_clu(k), device_id_type=MESH)
+
+    part = ids_half.at[pl.ds(0, 7)]
+    pltpu.make_async_copy(part, part, ids_rsem.at[0]).wait()
+    for k in range(1, 16):
+        there = lax.rem(vol + k, 16)
+        pltpu.make_async_remote_copy(
+            src_ref=ids_half.at[:, there],
+            dst_ref=ids_recv.at[vol],
+            send_sem=ids_ssem.at[1],
+            recv_sem=ids_rsem.at[1],
+            device_id=(clu, there),
+            device_id_type=MESH,
+        ).start()
+    ids_recv[vol] = ids_half[:, vol]
+
+    loads[3].wait()
     lane = iota((NVEC, LEAF), 1)
 
     def gather(c, carry):
@@ -197,46 +235,52 @@
 
     lax.fori_loop(0, CLUSTERS, gather, 0)
 
-    loads[0].wait()
-    loads[1].wait()
+    for load in loads[4:7]:
+        load.wait()
+    to_smem.wait()
     same = iota((8 * NVEC, 8 * RANK), 0) // NVEC == iota((8 * NVEC, 8 * RANK), 1) // RANK
-    terms[0] = jnp.zeros((NVEC, LEAF), BF16)
-
-    def far(g, carry):
-        first = g * 8
-        lhs = jnp.concatenate([bound[fsrc_ref[first + i]] for i in range(8)], axis=0)
-        v = fv_vm[pl.ds(first, 8)].reshape(8 * RANK, LEAF)
-        u = fu_vm[pl.ds(first, 8)].reshape(8 * RANK, LEAF)
+    me = clu * 16 + vol
+
+    def far(i):
+        devs = [partner(i * 2 + a, 1) for a in range(2)]
+        pairs = [
+            jnp.clip(idx_sm[j, dev[0] * 16 + dev[1]], 0, FAR - 1) for dev in devs for j in range(SLOTS)
+        ]
+        lhs = jnp.concatenate([bound[fsrc_ref[q]] for q in pairs], axis=0)
+        v = jnp.concatenate([fv_vm[q] for q in pairs], axis=0)
+        u = jnp.concatenate([fu_vm[q] for q in pairs], axis=0)
         coeff = lax.dot_general(lhs, v, NT, preferred_element_type=F32)
         coeff = jnp.where(same, coeff, 0.0).astype(BF16)
-        term = jnp.dot(coeff, u, preferred_element_type=F32)
-        terms[pl.ds(first + 1, 8)] = term.astype(BF16).reshape(8, NVEC, LEAF)
-        return carry
-
-    lax.fori_loop(0, FAR // 8, far, 0)
-
-    to_smem.wait()
-    me = clu * 16 + vol
-    for j in range(SLOTS):
-        recv[0, j * NVEC : (j + 1) * NVEC, :] = terms[jnp.clip(idx_sm[j, me], 0, FAR)]
-
-    def send_terms(k, carry):
-        dev, flat = partner(k)
-        for j in range(SLOTS):
-            send[k, j * NVEC : (j + 1) * NVEC, :] = terms[jnp.clip(idx_sm[j, flat], 0, FAR)]
+        term = jnp.dot(coeff, u, preferred_element_type=F32).astype(BF16)
+        return devs, term.reshape(2, SLOTS * NVEC, LEAF)
+
+    def send_term(k, dev):
         pltpu.make_async_remote_copy(
             src_ref=send.at[k],
             dst_ref=recv.at[k],
             send_sem=send_sem,
-            recv_sem=recv_sem.at[k // PER_STEP],
+            recv_sem=recv_sem.at[lax.div(k, PER_STEP)],
             device_id=dev,
             device_id_type=MESH,
         ).start()
+
+    devs, term = far(0)
+    recv[0] = term[0]
+    send[1] = term[1]
+    pl.semaphore_wait(sync, 7)
+    send_term(1, devs[1])
+
+    def far_step(i, carry):
+        devs, term = far(i)
+        send[pl.ds(i * 2, 2)] = term
+        for a in range(2):
+            send_term(i * 2 + a, devs[a])
         return carry
 
-    lax.fori_loop(1, NDEV, send_terms, 0)
-
-    loads[2].wait()
+    lax.fori_loop(1, NDEV // 2, far_step, 0, unroll=3)
+
+    for load in loads[7:]:
+        load.wait()
 
     def near(g, carry):
         first = g * 8
@@ -269,7 +313,7 @@
 
     lax.fori_loop(0, NEAR // 16, near_sum, 0)
 
-    before, after = (me + NDEV - 1) % NDEV, (me + 1) % NDEV
+    before, after = lax.rem(me + NDEV - 1, NDEV), lax.rem(me + 1, NDEV)
     near_copies = []
     for i, (block, to) in enumerate(((0, before), (2, after))):
         copy = pltpu.make_async_remote_copy(
@@ -277,19 +321,22 @@
             dst_ref=nrecv.at[i],
             send_sem=near_ssem.at[i],
             recv_sem=near_rsem.at[i],
-            device_id=(to // 16, to % 16),
+            device_id=(lax.div(to, 16), lax.rem(to, 16)),
             device_id_type=MESH,
         )
         copy.start()
         near_copies.append(copy)
 
-    pltpu.make_async_copy(ids_recv.at[pl.ds(1, NDEV - 1)], ids_recv.at[pl.ds(1, NDEV - 1)], ids_rsem).wait()
+    part = ids_recv.at[pl.ds(0, 15)]
+    pltpu.make_async_copy(part, part, ids_rsem.at[1]).wait()
     vec_same = iota((LEAF, LEAF), 0) % NVEC == iota((LEAF, LEAF), 1) % NVEC
     cluster_row = (iota((LEAF, LEAF), 0) // NVEC).astype(F32)
     left = iota((1, LEAF), 1) < LEAF // 2
 
     def make_mask(g, carry):
-        wanted = jnp.where(left, ids_recv[g * 2], ids_recv[g * 2 + 1])
+        origins = [partner(g * 2 + a, -1) for a in range(2)]
+        one, two = [ids_recv[origin[1], origin[0]] for origin in origins]
+        wanted = jnp.where(left, one, two)
         masks[g] = jnp.where(vec_same & (cluster_row == wanted), 1.0, 0.0).astype(BF16)
         return carry
 
@@ -312,8 +359,10 @@
 
     sent = table.at[pl.ds(0, 240)]
     pltpu.make_async_copy(sent, sent, tab_send).wait()
-    sent = ids_send.at[pl.ds(1, NDEV - 1)]
-    pltpu.make_async_copy(sent, sent, ids_ssem).wait()
+    sent = ids_half.at[pl.ds(0, 7)]
+    pltpu.make_async_copy(sent, sent, ids_ssem.at[0]).wait()
+    sent = ids_recv.at[pl.ds(0, 15)]
+    pltpu.make_async_copy(sent, sent, ids_ssem.at[1]).wait()
     sent = send.at[pl.ds(1, NDEV - 1)]
     pltpu.make_async_copy(sent, sent, send_sem).wait()
 
@@ -332,38 +381,46 @@
     far_cluster,
 ):
     vmem = pl.BlockSpec(memory_space=pltpu.VMEM)
-    smem = pl.BlockSpec(memory_space=pltpu.SMEM)
-    hbm = pl.BlockSpec(memory_space=pl.ANY)
+    hbm = pl.BlockSpec(memory_space=pltpu.HBM)
     dma = pltpu.SemaphoreType.DMA
     return pl.pallas_call(
         kernel,
         out_shape=jax.ShapeDtypeStruct((CLUSTERS, NVEC, LEAF), F32),
-        in_specs=[vmem, smem, smem, vmem, vmem, smem, vmem, vmem, hbm, hbm, hbm],
+        in_specs=[hbm] * 11,
         out_specs=vmem,
         scratch_shapes=[
+            pltpu.VMEM((NVEC, TILES // 16 * LEAF), BF16),
+            pltpu.SMEM((CLUSTERS, LEAF), jnp.int32),
+            pltpu.SMEM((NEAR,), jnp.int32),
+            pltpu.VMEM((1, NEAR), jnp.int32),
+            pltpu.VMEM((1, NEAR), jnp.int32),
+            pltpu.SMEM((FAR,), jnp.int32),
+            pltpu.VMEM((1, FAR), jnp.int32),
+            pltpu.VMEM((1, FAR), jnp.int32),
             pltpu.VMEM((TILES, NVEC, LEAF), BF16),
             pltpu.VMEM((NEAR, LEAF, LEAF), BF16),
             pltpu.VMEM((FAR, RANK, LEAF), BF16),
             pltpu.VMEM((FAR, RANK, LEAF), BF16),
             pltpu.VMEM((CLUSTERS, NVEC, LEAF), BF16),
-            pltpu.VMEM((FAR + 8, NVEC, LEAF), BF16),
             pltpu.VMEM((NDEV, SLOTS * NVEC, LEAF), BF16),
             pltpu.VMEM((NDEV, SLOTS * NVEC, LEAF), BF16),
             pltpu.VMEM((8, NDEV), jnp.int32),
             pltpu.SMEM((8, NDEV), jnp.int32),
             pltpu.VMEM((NDEV, 1, LEAF), F32),
-            pltpu.VMEM((NDEV, 1, LEAF), F32),
+            pltpu.VMEM((8, 16, 1, LEAF), F32),
+            pltpu.VMEM((16, 8, 1, LEAF), F32),
             pltpu.VMEM((NDEV // 2, LEAF, LEAF), BF16),
             pltpu.VMEM((NEAR, NVEC, LEAF), BF16),
             pltpu.VMEM((NEAR, NVEC, LEAF), BF16),
             pltpu.VMEM((3 * CLUSTERS, NVEC, LEAF), F32),
             pltpu.VMEM((2, CLUSTERS, NVEC, LEAF), F32),
-            dma((3,)),
+            dma((11,)),
             dma,
             dma,
             dma((32,)),
-            dma,
-            dma,
+            dma((2,)),
+            dma((2,)),
+            pltpu.SemaphoreType.REGULAR,
             dma,
             dma((STEPS,)),
             dma((2,)),
@@ -374,6 +431,7 @@
         ),
         cost_estimate=pl.CostEstimate(flops=2 * 10**8, bytes_accessed=9 * 2**20, transcendentals=0),
     )(
+        *(pltpu.with_memory_space_constraint(a, pltpu.HBM) for a in (
         volume_field,
         trace_rows,
         near_source,
@@ -385,7 +443,7 @@
         near_block,
         far_v,
         far_u,
-    )
+    )))
 
 
 def solution(mesh):

time: 78.6 us -> 55.4 us (0.70)
  Pallas kernels: 66.7 us -> 53.8 us
  local copies, waits for them, and re-layouts: 11.5 us -> 0.63 us
    pallas_call x1, Pallas kernels: 66.7 us -> 53.8 us  [body(): pl.pallas_call(kernel, out_shape=jax.ShapeDtypeStruct((CLUSTERS, NVEC, LE...]
    unnamed x23 -> x1, local copies, waits for them, and re-layouts: 11.5 us -> 0.63 us
where the time goes in v2:
time: 55.4 us; the launch traced here: 54.5 us
  Pallas kernels  53.8 us (97%)
  local copies, waits for them, and re-layouts  0.63 us (1%)
    pallas_call x1, Pallas kernels, body(): pl.pallas_call(kernel, out_shape=jax.ShapeDtypeStruct((CLUSTERS, NVEC, LE...  53.8 us

profile of v2, /device:TPU:1, one launch (start us, length us, event | category | flops | bytes accessed | tf_op | source)
XLA Modules:
  0.0 54.5 jit_solution(3709346930794086792)
XLA Ops:
  0.0 53.8 %shard_map.109 = f32[8,16,128]{2,1,0:T(8,128)S(1)} custom-call(bf16[16,2048]{1,0:T(8,128)(2,1)} %vol_hbm.1, s32[8,128]{1,0:T(8,128)} %rows_hbm.1, s32[128]{0:T(128)} %nsrc_hbm.1, s32[1,128]{1,0:T(1,128)} %bitcast.6, s32[1,128]{1,0:T(1,128)} %bitcast.7, s32[256]{0:T(256)} %fsrc_hbm.1, s32[1,256]{1,0:T(1,128)} %bitcast.4, s32[1,256]{1,0:T(1,128)} %bitcast.5, ...), custom_call_target="tpu_custom_call" | custom-call | flops 200000000 | bytes 9437184 | tf_op jit(solution)/shard_map/pallas_call | solution.py:386
  53.9 0.6 %copy.13 = f32[8,16,128]{2,1,0:T(8,128)} copy(f32[8,16,128]{2,1,0:T(8,128)S(1)} %shard_map.109) | data formatting | bytes 131072

commit v3 on v2

--- a/solution.py
+++ b/solution.py
@@ -19,7 +19,8 @@
 FAR = 256
 RANK = 32
 STEPS = 16
-PER_STEP = NDEV // STEPS
+SPLIT = 4
+HALF = 8
 TILES = 256
 
 
@@ -32,14 +33,25 @@
     return lax.div(clu, 2), lax.rem(clu, 2), lax.div(vol, 4), lax.rem(vol, 4)
 
 
-def partner(k, sign):
+def at(dx, dcore, dy, dz):
     x, core, y, z = place()
-    m = lax.rem(k * 37, NDEV)
-    r = lax.div(m, 2)
-    dx, dy, dz = lax.rem(r, 4), lax.rem(lax.div(r, 4), 4), lax.div(r, 16)
-    clu = lax.rem(x + 4 + sign * dx, 4) * 2 + lax.rem(core + m, 2)
-    vol = lax.rem(y + 4 + sign * dy, 4) * 4 + lax.rem(z + 4 + sign * dz, 4)
-    return clu, vol
+    clu = lax.rem(x + dx, 4) * 2 + lax.rem(core + dcore, 2)
+    return clu, lax.rem(y + dy, 4) * 4 + lax.rem(z + dz, 4)
+
+
+def member(s, g):
+    return at(lax.div(g, 2), lax.rem(g, 2), 0, 0) if s < HALF else at(0, lax.rem(g, 2), lax.div(g, 2), 0)
+
+
+def offset(along_y, p):
+    if along_y:
+        return lax.rem(lax.div(p, 2) + 1, 4), 1 + 2 * lax.rem(p, 2)
+    return lax.rem(p + 1, 4), 2 - 2 * lax.div(p, 4)
+
+
+def owner(along_y, g, p):
+    d, dz = offset(along_y, p)
+    return at(d, lax.rem(g, 2), lax.div(g, 2), dz) if along_y else at(lax.div(g, 2), lax.rem(g, 2), d, dz)
 
 
 def kernel(
@@ -70,10 +82,12 @@
     bound,
     send,
     recv,
+    wide_send,
+    wide_recv,
     idx_vm,
     idx_sm,
+    ids_all,
     ids_send,
-    ids_half,
     ids_recv,
     masks,
     nterm_hi,
@@ -86,9 +100,10 @@
     tab_recv,
     ids_ssem,
     ids_rsem,
-    sync,
     send_sem,
     recv_sem,
+    wide_ssem,
+    wide_rsem,
     near_ssem,
     near_rsem,
 ):
@@ -104,7 +119,7 @@
         return clu, lax.rem(y + ey, 4) * 4 + lax.rem(z + ez, 4)
 
     near_by = [along_clu(k) for k in range(1, 8)]
-    near_by += [along(e, 0) for e in range(1, 4)] + [along(0, e) for e in range(1, 4)]
+    near_by += [at(0, c, e, 0) for c in range(2) for e in range(1, 4)] + [along(0, e) for e in range(1, 4)]
     for dev in near_by:
         pl.semaphore_signal(barrier, inc=1, device_id=dev, device_id_type=MESH)
 
@@ -144,7 +159,16 @@
         idx_vm[j : j + 1, :] = found[0:1, :].astype(jnp.int32)
         target = jnp.sum(chosen * clusters, axis=1, keepdims=True) - 1.0
         ids = jnp.where(slot_of_lane == j, target, ids)
-    ids_send[...] = ids.reshape(NDEV, 1, LEAF)
+    ids_all[...] = ids.reshape(NDEV, 1, LEAF)
+    for s in (0, HALF):
+        for g in range(8):
+
+            def ids_row(p, carry, s=s, g=g):
+                dev = owner(s >= HALF, g, p)
+                ids_send[s + g, p] = ids_all[dev[0] * 16 + dev[1]]
+                return carry
+
+            lax.fori_loop(0, HALF, ids_row, 0, unroll=4)
     to_smem = pltpu.make_async_copy(idx_vm, idx_sm, idx_sem)
     to_smem.start()
 
@@ -169,7 +193,10 @@
         block = half(dy, dz, h)
         pltpu.make_async_copy(block, block, tab_recv.at[h * 16 + dy * 4 + dz]).wait()
 
-    order = (1, 3, 2)
+    def mirrored(e):
+        return lax.rem(e + core * (4 - 2 * e), 4)
+
+    order = [mirrored(e) for e in (1, 3, 2)]
     for e in order:
         pass_on(0, 0, 0, 0, e)
         pass_on(0, 0, 1, e, 0)
@@ -177,17 +204,17 @@
         pass_on(0, 0, 0, e, 0)
         pass_on(0, 0, 1, 0, e)
 
-    for k in range(1, 8):
-        dev = along_clu(k)
-        pltpu.make_async_remote_copy(
-            src_ref=ids_send.at[pl.ds(dev[0] * 16, 16)],
-            dst_ref=ids_half.at[clu],
-            send_sem=ids_ssem.at[0],
-            recv_sem=ids_rsem.at[0],
-            device_id=dev,
-            device_id_type=MESH,
-        ).start()
-    ids_half[clu] = ids_send[pl.ds(clu * 16, 16)]
+    for s in (0, HALF):
+        for g in range(1, 8):
+            pltpu.make_async_remote_copy(
+                src_ref=ids_send.at[s + g],
+                dst_ref=ids_recv.at[s + g],
+                send_sem=ids_ssem,
+                recv_sem=ids_rsem,
+                device_id=member(s, g),
+                device_id_type=MESH,
+            ).start()
+        ids_recv[s] = ids_send[s]
 
     for d in order:
         arrived(0, d, 0)
@@ -196,6 +223,22 @@
         arrived(d, 0, 1)
         for e in order:
             pass_on(d, 0, 1, 0, e)
+    part = ids_recv.at[pl.ds(0, 14)]
+    pltpu.make_async_copy(part, part, ids_rsem).wait()
+    vec_same = iota((LEAF, LEAF), 0) % NVEC == iota((LEAF, LEAF), 1) % NVEC
+    cluster_row = (iota((LEAF, LEAF), 0) // NVEC).astype(F32)
+    left = iota((1, LEAF), 1) < LEAF // 2
+
+    def make_mask(p, carry):
+        for s in (0, HALF):
+            for a in range(4):
+                wanted = jnp.where(left, ids_recv[s + 2 * a, p], ids_recv[s + 2 * a + 1, p])
+                pick = jnp.where(vec_same & (cluster_row == wanted), 1.0, 0.0)
+                masks[s + p, :, a * LEAF : (a + 1) * LEAF] = pick.astype(BF16)
+        return carry
+
+    lax.fori_loop(0, HALF, make_mask, 0)
+
     for d in order:
         arrived(d, 0, 0)
         arrived(0, d, 1)
@@ -203,23 +246,6 @@
         for e in order:
             arrived(d, e, 0)
             arrived(d, e, 1)
-
-    for k in range(1, 8):
-        pl.semaphore_signal(sync, inc=1, device_id=along_clu(k), device_id_type=MESH)
-
-    part = ids_half.at[pl.ds(0, 7)]
-    pltpu.make_async_copy(part, part, ids_rsem.at[0]).wait()
-    for k in range(1, 16):
-        there = lax.rem(vol + k, 16)
-        pltpu.make_async_remote_copy(
-            src_ref=ids_half.at[:, there],
-            dst_ref=ids_recv.at[vol],
-            send_sem=ids_ssem.at[1],
-            recv_sem=ids_rsem.at[1],
-            device_id=(clu, there),
-            device_id_type=MESH,
-        ).start()
-    ids_recv[vol] = ids_half[:, vol]
 
     loads[3].wait()
     lane = iota((NVEC, LEAF), 1)
@@ -239,10 +265,8 @@
         load.wait()
     to_smem.wait()
     same = iota((8 * NVEC, 8 * RANK), 0) // NVEC == iota((8 * NVEC, 8 * RANK), 1) // RANK
-    me = clu * 16 + vol
-
-    def far(i):
-        devs = [partner(i * 2 + a, 1) for a in range(2)]
+
+    def far(devs):
         pairs = [
             jnp.clip(idx_sm[j, dev[0] * 16 + dev[1]], 0, FAR - 1) for dev in devs for j in range(SLOTS)
         ]
@@ -252,32 +276,61 @@
         coeff = lax.dot_general(lhs, v, NT, preferred_element_type=F32)
         coeff = jnp.where(same, coeff, 0.0).astype(BF16)
         term = jnp.dot(coeff, u, preferred_element_type=F32).astype(BF16)
-        return devs, term.reshape(2, SLOTS * NVEC, LEAF)
-
-    def send_term(k, dev):
+        return term.reshape(2, SLOTS * NVEC, LEAF)
+
+    def members():
+        for h in range(4):
+            for s in (0, HALF):
+                yield s, h, mirrored(h if s == 0 else (4 - h) % 4) * 2
+
+    def far_step(p, carry):
+        for s, h, first in members():
+            term = far([owner(s >= HALF, first + c, p) for c in range(2)])
+            if h == 0:
+                recv[s + p, 0] = term[0]
+                send[s + p, 1] = term[1]
+            else:
+                send[s + p, pl.ds(first, 2)] = term
+        for s, h, first in members():
+            for c in range(2):
+                if h + c == 0:
+                    continue
+                g = first + c
+                pltpu.make_async_remote_copy(
+                    src_ref=send.at[s + p, g],
+                    dst_ref=recv.at[s + p, g],
+                    send_sem=send_sem,
+                    recv_sem=recv_sem.at[s + p],
+                    device_id=member(s, g),
+                    device_id_type=MESH,
+                ).start()
+        return carry
+
+    lax.fori_loop(0, HALF, far_step, 0)
+
+    def line_sum(s, p):
+        part = recv.at[s + p, pl.ds(1, 7)]
+        pltpu.make_async_copy(part, part, recv_sem.at[s + p]).wait()
+        block = recv[s + p].reshape(8 * SLOTS * NVEC, LEAF)
+        return jnp.dot(masks[s + p], block, preferred_element_type=F32)
+
+    def merge(s, p):
+        wide_send[s + p] = line_sum(s, p)
         pltpu.make_async_remote_copy(
-            src_ref=send.at[k],
-            dst_ref=recv.at[k],
-            send_sem=send_sem,
-            recv_sem=recv_sem.at[lax.div(k, PER_STEP)],
-            device_id=dev,
+            src_ref=wide_send.at[s + p],
+            dst_ref=wide_recv.at[s + p],
+            send_sem=wide_ssem,
+            recv_sem=wide_rsem.at[s + p],
+            device_id=owner(s >= HALF, 0, p),
             device_id_type=MESH,
         ).start()
 
-    devs, term = far(0)
-    recv[0] = term[0]
-    send[1] = term[1]
-    pl.semaphore_wait(sync, 7)
-    send_term(1, devs[1])
-
-    def far_step(i, carry):
-        devs, term = far(i)
-        send[pl.ds(i * 2, 2)] = term
-        for a in range(2):
-            send_term(i * 2 + a, devs[a])
+    def merge_step(p, carry):
+        merge(0, p)
+        merge(HALF, p)
         return carry
 
-    lax.fori_loop(1, NDEV // 2, far_step, 0, unroll=3)
+    lax.fori_loop(0, SPLIT, merge_step, 0)
 
     for load in loads[7:]:
         load.wait()
@@ -313,6 +366,7 @@
 
     lax.fori_loop(0, NEAR // 16, near_sum, 0)
 
+    me = clu * 16 + vol
     before, after = lax.rem(me + NDEV - 1, NDEV), lax.rem(me + 1, NDEV)
     near_copies = []
     for i, (block, to) in enumerate(((0, before), (2, after))):
@@ -327,44 +381,28 @@
         copy.start()
         near_copies.append(copy)
 
-    part = ids_recv.at[pl.ds(0, 15)]
-    pltpu.make_async_copy(part, part, ids_rsem.at[1]).wait()
-    vec_same = iota((LEAF, LEAF), 0) % NVEC == iota((LEAF, LEAF), 1) % NVEC
-    cluster_row = (iota((LEAF, LEAF), 0) // NVEC).astype(F32)
-    left = iota((1, LEAF), 1) < LEAF // 2
-
-    def make_mask(g, carry):
-        origins = [partner(g * 2 + a, -1) for a in range(2)]
-        one, two = [ids_recv[origin[1], origin[0]] for origin in origins]
-        wanted = jnp.where(left, one, two)
-        masks[g] = jnp.where(vec_same & (cluster_row == wanted), 1.0, 0.0).astype(BF16)
-        return carry
-
-    lax.fori_loop(0, NDEV // 2, make_mask, 0)
-
-    total = nsum[pl.ds(CLUSTERS, CLUSTERS)].reshape(CLUSTERS * NVEC, LEAF)
-    for s in range(STEPS):
-        lo = max(1, s * PER_STEP)
-        part = recv.at[pl.ds(lo, (s + 1) * PER_STEP - lo)]
-        pltpu.make_async_copy(part, part, recv_sem.at[s]).wait()
-        for t in range(PER_STEP // 4):
-            g = s * PER_STEP // 2 + t * 2
-            pick = jnp.concatenate([masks[g], masks[g + 1]], axis=1)
-            block = recv[pl.ds(g * 2, 4)].reshape(4 * SLOTS * NVEC, LEAF)
-            total += jnp.dot(pick, block, preferred_element_type=F32)
+    lax.fori_loop(SPLIT, HALF - 1, merge_step, 0)
+    merge(HALF, HALF - 1)
+    total = line_sum(0, HALF - 1) + nsum[pl.ds(CLUSTERS, CLUSTERS)].reshape(CLUSTERS * NVEC, LEAF)
     for copy in near_copies:
         copy.wait()
-    total = total.reshape(CLUSTERS, NVEC, LEAF)
-    out_ref[...] = total + nrecv[0] + nrecv[1]
+    total += (nrecv[0] + nrecv[1]).reshape(CLUSTERS * NVEC, LEAF)
+    for p in range(HALF):
+        for s in (0, HALF):
+            if s + p != HALF - 1:
+                part = wide_recv.at[s + p]
+                pltpu.make_async_copy(part, part, wide_rsem.at[s + p]).wait()
+                total += wide_recv[s + p]
+    out_ref[...] = total.reshape(CLUSTERS, NVEC, LEAF)
 
     sent = table.at[pl.ds(0, 240)]
     pltpu.make_async_copy(sent, sent, tab_send).wait()
-    sent = ids_half.at[pl.ds(0, 7)]
-    pltpu.make_async_copy(sent, sent, ids_ssem.at[0]).wait()
-    sent = ids_recv.at[pl.ds(0, 15)]
-    pltpu.make_async_copy(sent, sent, ids_ssem.at[1]).wait()
-    sent = send.at[pl.ds(1, NDEV - 1)]
+    sent = ids_recv.at[pl.ds(0, 14)]
+    pltpu.make_async_copy(sent, sent, ids_ssem).wait()
+    sent = send.at[pl.ds(0, 14)]
     pltpu.make_async_copy(sent, sent, send_sem).wait()
+    sent = wide_send.at[pl.ds(0, 15)]
+    pltpu.make_async_copy(sent, sent, wide_ssem).wait()
 
 
 def body(
@@ -402,14 +440,16 @@
             pltpu.VMEM((FAR, RANK, LEAF), BF16),
             pltpu.VMEM((FAR, RANK, LEAF), BF16),
             pltpu.VMEM((CLUSTERS, NVEC, LEAF), BF16),
-            pltpu.VMEM((NDEV, SLOTS * NVEC, LEAF), BF16),
-            pltpu.VMEM((NDEV, SLOTS * NVEC, LEAF), BF16),
+            pltpu.VMEM((STEPS, 8, SLOTS * NVEC, LEAF), BF16),
+            pltpu.VMEM((STEPS, 8, SLOTS * NVEC, LEAF), BF16),
+            pltpu.VMEM((STEPS, LEAF, LEAF), F32),
+            pltpu.VMEM((STEPS, LEAF, LEAF), F32),
             pltpu.VMEM((8, NDEV), jnp.int32),
             pltpu.SMEM((8, NDEV), jnp.int32),
             pltpu.VMEM((NDEV, 1, LEAF), F32),
-            pltpu.VMEM((8, 16, 1, LEAF), F32),
-            pltpu.VMEM((16, 8, 1, LEAF), F32),
-            pltpu.VMEM((NDEV // 2, LEAF, LEAF), BF16),
+            pltpu.VMEM((STEPS, HALF, 1, LEAF), F32),
+            pltpu.VMEM((STEPS, HALF, 1, LEAF), F32),
+            pltpu.VMEM((STEPS, LEAF, 8 * SLOTS * NVEC), BF16),
             pltpu.VMEM((NEAR, NVEC, LEAF), BF16),
             pltpu.VMEM((NEAR, NVEC, LEAF), BF16),
             pltpu.VMEM((3 * CLUSTERS, NVEC, LEAF), F32),
@@ -418,9 +458,10 @@
             dma,
             dma,
             dma((32,)),
-            dma((2,)),
-            dma((2,)),
-            pltpu.SemaphoreType.REGULAR,
+            dma,
+            dma,
+            dma,
+            dma((STEPS,)),
             dma,
             dma((STEPS,)),
             dma((2,)),

time: 55.4 us -> 47.7 us (0.86); the launches traced: 54.5 us -> 47.6 us
  Pallas kernels: 53.8 us -> 47 us
    pallas_call x1, Pallas kernels: 53.8 us -> 47 us  [body(): pl.pallas_call(kernel, out_shape=jax.ShapeDtypeStruct((CLUSTERS, NVEC, LE...]
where the time goes in v3:
time: 47.7 us; the launch traced here: 47.6 us
  Pallas kernels  47 us (99%)
  local copies, waits for them, and re-layouts  0.63 us (1%)
    pallas_call x1, Pallas kernels, body(): pl.pallas_call(kernel, out_shape=jax.ShapeDtypeStruct((CLUSTERS, NVEC, LE...  47 us

profile of v3, /device:TPU:1, one launch (start us, length us, event | category | flops | bytes accessed | tf_op | source)
XLA Modules:
  0.0 47.6 jit_solution(12305694432830204517)
XLA Ops:
  0.0 47.0 %shard_map.109 = f32[8,16,128]{2,1,0:T(8,128)S(1)} custom-call(bf16[16,2048]{1,0:T(8,128)(2,1)} %vol_hbm.1, s32[8,128]{1,0:T(8,128)} %rows_hbm.1, s32[128]{0:T(128)} %nsrc_hbm.1, s32[1,128]{1,0:T(1,128)} %bitcast.6, s32[1,128]{1,0:T(1,128)} %bitcast.7, s32[256]{0:T(256)} %fsrc_hbm.1, s32[1,256]{1,0:T(1,128)} %bitcast.4, s32[1,256]{1,0:T(1,128)} %bitcast.5, ...), custom_call_target="tpu_custom_call" | custom-call | flops 200000000 | bytes 9437184 | tf_op jit(solution)/shard_map/pallas_call | solution.py:424
  47.0 0.6 %copy.13 = f32[8,16,128]{2,1,0:T(8,128)} copy(f32[8,16,128]{2,1,0:T(8,128)S(1)} %shard_map.109) | data formatting | bytes 131072

commit v4 on v3

--- a/solution.py
+++ b/solution.py
@@ -19,7 +19,7 @@
 FAR = 256
 RANK = 32
 STEPS = 16
-SPLIT = 4
+LAG = 4
 HALF = 8
 TILES = 256
 
@@ -306,8 +306,6 @@
                 ).start()
         return carry
 
-    lax.fori_loop(0, HALF, far_step, 0)
-
     def line_sum(s, p):
         part = recv.at[s + p, pl.ds(1, 7)]
         pltpu.make_async_copy(part, part, recv_sem.at[s + p]).wait()
@@ -330,11 +328,6 @@
         merge(HALF, p)
         return carry
 
-    lax.fori_loop(0, SPLIT, merge_step, 0)
-
-    for load in loads[7:]:
-        load.wait()
-
     def near(g, carry):
         first = g * 8
         for i in range(8):
@@ -344,14 +337,13 @@
             nterm_lo[first + i] = (term - high.astype(F32)).astype(BF16)
         return carry
 
-    lax.fori_loop(0, NEAR // 8, near, 0)
-
+    for load in loads[7:]:
+        load.wait()
     rows = 3 * CLUSTERS * NVEC
     named = (noff_ref[...] * CLUSTERS + nclu_ref[...]).astype(F32).astype(BF16)
     named = jnp.broadcast_to(named, (16, NEAR))
     vec_row = iota((rows, 256), 0) % NVEC == iota((rows, 256), 1) % NVEC
     target_row = (iota((rows, 256), 0) // NVEC).astype(F32)
-    nsum[...] = jnp.zeros_like(nsum)
 
     def near_sum(g, carry):
         first = g * 16
@@ -364,8 +356,26 @@
         nsum[...] += total.reshape(3 * CLUSTERS, NVEC, LEAF)
         return carry
 
-    lax.fori_loop(0, NEAR // 16, near_sum, 0)
-
+    def near_piece(q):
+        near(2 * q, 0)
+        near(2 * q + 1, 0)
+        near_sum(q, 0)
+
+    def both_steps(p, carry):
+        far_step(p, carry)
+        near_piece(p - LAG)
+        return merge_step(p - LAG, carry)
+
+    lax.fori_loop(0, LAG, far_step, 0)
+    nsum[...] = jnp.zeros_like(nsum)
+    lax.fori_loop(LAG, HALF, both_steps, 0)
+
+    def late_steps(p, carry):
+        near_piece(p)
+        return merge_step(p, carry)
+
+    lax.fori_loop(HALF - LAG, HALF - 1, late_steps, 0)
+    near_piece(HALF - 1)
     me = clu * 16 + vol
     before, after = lax.rem(me + NDEV - 1, NDEV), lax.rem(me + 1, NDEV)
     near_copies = []
@@ -381,7 +391,6 @@
         copy.start()
         near_copies.append(copy)
 
-    lax.fori_loop(SPLIT, HALF - 1, merge_step, 0)
     merge(HALF, HALF - 1)
     total = line_sum(0, HALF - 1) + nsum[pl.ds(CLUSTERS, CLUSTERS)].reshape(CLUSTERS * NVEC, LEAF)
     for copy in near_copies:

time: 47.7 us -> 45.5 us (0.954)
  Pallas kernels: 47 us -> 44.8 us
    pallas_call x1, Pallas kernels: 47 us -> 44.8 us  [body(): pl.pallas_call(kernel, out_shape=jax.ShapeDtypeStruct((CLUSTERS, NVEC, LE...]
where the time goes in v4:
time: 45.5 us; the launch traced here: 45.4 us
  Pallas kernels  44.8 us (98%)
  local copies, waits for them, and re-layouts  0.63 us (1%)
    pallas_call x1, Pallas kernels, body(): pl.pallas_call(kernel, out_shape=jax.ShapeDtypeStruct((CLUSTERS, NVEC, LE...  44.8 us

profile of v4, /device:TPU:1, one launch (start us, length us, event | category | flops | bytes accessed | tf_op | source)
XLA Modules:
  0.0 45.4 jit_solution(2537302940256755676)
XLA Ops:
  0.0 44.8 %shard_map.109 = f32[8,16,128]{2,1,0:T(8,128)S(1)} custom-call(bf16[16,2048]{1,0:T(8,128)(2,1)} %vol_hbm.1, s32[8,128]{1,0:T(8,128)} %rows_hbm.1, s32[128]{0:T(128)} %nsrc_hbm.1, s32[1,128]{1,0:T(1,128)} %bitcast.6, s32[1,128]{1,0:T(1,128)} %bitcast.7, s32[256]{0:T(256)} %fsrc_hbm.1, s32[1,256]{1,0:T(1,128)} %bitcast.4, s32[1,256]{1,0:T(1,128)} %bitcast.5, ...), custom_call_target="tpu_custom_call" | custom-call | flops 200000000 | bytes 9437184 | tf_op jit(solution)/shard_map/pallas_call | solution.py:433
  44.8 0.6 %copy.13 = f32[8,16,128]{2,1,0:T(8,128)} copy(f32[8,16,128]{2,1,0:T(8,128)S(1)} %shard_map.109) | data formatting | bytes 131072

commit v5 on v4

--- a/solution.py
+++ b/solution.py
@@ -196,7 +196,7 @@
     def mirrored(e):
         return lax.rem(e + core * (4 - 2 * e), 4)
 
-    order = [mirrored(e) for e in (1, 3, 2)]
+    order = [mirrored(e) for e in (2, 1, 3)]
     for e in order:
         pass_on(0, 0, 0, 0, e)
         pass_on(0, 0, 1, e, 0)

time: 45.5 us -> 45.1 us (level)
  Pallas kernels: 44.8 us -> 44.3 us
where the time goes in v5:
time: 45.1 us; the launch traced here: 45 us
  Pallas kernels  44.3 us (98%)
  local copies, waits for them, and re-layouts  0.63 us (1%)
    pallas_call x1, Pallas kernels, body(): pl.pallas_call(kernel, out_shape=jax.ShapeDtypeStruct((CLUSTERS, NVEC, LE...  44.3 us

profile of v5, /device:TPU:1, one launch (start us, length us, event | category | flops | bytes accessed | tf_op | source)
XLA Modules:
  0.0 45.0 jit_solution(10016318582829627449)
XLA Ops:
  0.0 44.3 %shard_map.109 = f32[8,16,128]{2,1,0:T(8,128)S(1)} custom-call(bf16[16,2048]{1,0:T(8,128)(2,1)} %vol_hbm.1, s32[8,128]{1,0:T(8,128)} %rows_hbm.1, s32[128]{0:T(128)} %nsrc_hbm.1, s32[1,128]{1,0:T(1,128)} %bitcast.6, s32[1,128]{1,0:T(1,128)} %bitcast.7, s32[256]{0:T(256)} %fsrc_hbm.1, s32[1,256]{1,0:T(1,128)} %bitcast.4, s32[1,256]{1,0:T(1,128)} %bitcast.5, ...), custom_call_target="tpu_custom_call" | custom-call | flops 200000000 | bytes 9437184 | tf_op jit(solution)/shard_map/pallas_call | solution.py:433
  44.4 0.6 %copy.13 = f32[8,16,128]{2,1,0:T(8,128)} copy(f32[8,16,128]{2,1,0:T(8,128)S(1)} %shard_map.109) | data formatting | bytes 131072
